TPU v7x, 128 devices: a whole 4x4x4 slice. The times are simulated.
128 devices in a mesh: tm: 4 (over x_hi, core), space: 32 (over z, y, x_lo).
Axes of the slice: x: 4 (x_hi: 2, x_lo: 2; x = x_hi * 2 + x_lo), y: 4, z: 4, core: 2. Of those that a mesh axis runs over, the one named last changes fastest.
Arguments:
- vorticity: float32 [128, 2048, 2048], P('tm', 'space'), may hold values from -6 to 6
Outputs:
- spectrum: float32 [128, 256, 256], P(None, ('tm', 'space'))
All inputs are finite; a program needn't handle non-finite values.
Results may differ from a plain program's by a relative error of at most 0.000071.
Values sent between devices are 32-bit elements; how exact they have to be, the bound alone decides.
A program may use at most 128 MiB of HBM per device.

v0:
```python
import functools

import jax
import jax.numpy as jnp
import ml_dtypes
import numpy as np
from jax import lax
from jax.experimental import pallas as pl
from jax.experimental.pallas import tpu as pltpu
from jax.sharding import PartitionSpec as P

N = 2048
T_SIZE = 128
K = 256
MESH = pl.DeviceIdType.MESH
F32, BF16 = jnp.float32, jnp.bfloat16
STEPS = 8


def halves(a):
    hi = a.astype(np.float32).astype(ml_dtypes.bfloat16)
    lo = (a - hi.astype(np.float64)).astype(np.float32).astype(ml_dtypes.bfloat16)
    return np.stack([hi, lo])


def turn(product, period):
    angle = (product % period) * (2.0 * np.pi / period)
    return np.cos(angle), np.sin(angle)


@functools.cache
def tables():
    cell = np.arange(N // 2)[:, None]
    rows = []
    for parity in range(2):
        c, s = turn(cell * (2 * np.arange(K // 2) + parity)[None, :], N)
        rows.append(halves(np.concatenate([c, -s], axis=1)))
    rows = np.stack(rows)
    columns = []
    for half in range(2):
        b, x, tm, a, i = np.meshgrid(
            np.arange(4), np.arange(2), np.arange(4), np.arange(4), np.arange(2), indexing="ij"
        )
        z, y = (a, b) if half == 0 else (b, a)
        wave = (64 * tm + 16 * z + 4 * y + 2 * x + i - K // 2).reshape(-1, 1)
        sets = []
        for own_b in range(4):
            for own_x in range(2):
                src, r = np.meshgrid(np.arange(4), np.arange(64), indexing="ij")
                z, y = (src, own_b) if half == 0 else (own_b, src)
                grid = (64 * (8 * z + 2 * y + own_x) + r).reshape(1, -1)
                c, s = turn(wave * grid, N)
                sets.append(halves(np.concatenate([c, s], axis=0)))
        columns.append(np.stack(sets))
    t = np.arange(T_SIZE)
    taper = 0.5 - 0.5 * np.cos(2.0 * np.pi * t / T_SIZE)
    scale = taper / N / np.sqrt(np.sum(taper * taper))
    tm, a, j = np.meshgrid(np.arange(4), np.arange(4), np.arange(8), indexing="ij")
    when = (32 * tm + 4 * j + a).reshape(-1)
    c, s = turn(np.arange(T_SIZE)[:, None] * when[None, :], T_SIZE)
    eye = np.eye(2)
    time = halves(
        np.concatenate([np.kron(c * scale[when], eye), np.kron(s * scale[when], eye)], axis=0)
    )
    perm = np.zeros((K, K))
    k = np.arange(K)
    perm[(k % 2) * 128 + k // 2, k] = 1.0
    return rows, columns[0], columns[1], time, perm.astype(ml_dtypes.bfloat16)


def split(v):
    hi = v.astype(BF16)
    return hi, (v - hi.astype(F32)).astype(BF16)


def dot(a, b):
    return jnp.dot(a, b, preferred_element_type=F32)


def turned(table_hi, table_lo, data):
    hi, lo = split(data)
    both = dot(table_hi, hi) + dot(table_hi, lo) + dot(table_lo, hi)
    top, low = both[:256], both[256:]
    return top[:, :128] + low[:, 128:], top[:, 128:] - low[:, :128]


def kernel(
    v_ref, rows_ref, cola_ref, colb_ref, time_ref, perm_ref, o_ref,
    vbuf, rows, cols, time, perm,
    send1, recv1, part, hrecv, qrecv, xsend, xkeep, xrecv, fsend, frecv,
    v_sem, c_sem, s1_send, s1_recv, h_send, h_recv, q_send, q_recv, x_send, x_recv, f_send, f_recv,
):
    tm = lax.axis_index("tm")
    me = lax.axis_index("space")
    z, y, x = me // 8, (me // 2) % 4, me % 2
    first = (z, y)
    second = (y, z)

    def space(half, a, b, xx):
        return (a * 4 + b) * 2 + xx if half == 0 else (b * 4 + a) * 2 + xx

    def ring(v, d):
        return (v + d) % 4

    tables_in = [
        pltpu.make_async_copy(rows_ref, rows, c_sem.at[0]),
        pltpu.make_async_copy(cola_ref.at[y * 2 + x], cols.at[0], c_sem.at[1]),
        pltpu.make_async_copy(colb_ref.at[z * 2 + x], cols.at[1], c_sem.at[2]),
        pltpu.make_async_copy(time_ref, time, c_sem.at[3]),
        pltpu.make_async_copy(perm_ref, perm, c_sem.at[4]),
    ]

    def fetch(j):
        return pltpu.make_async_copy(v_ref.at[pl.ds(4 * j, 4)], vbuf.at[pl.ds(4 * j, 4)], v_sem.at[j])

    tables_in[0].start()
    for j in range(STEPS):
        fetch(j).start()
    for copy in tables_in[1:]:
        copy.start()

    barrier = pltpu.get_barrier_semaphore()

    def greet(tm_to, space_to):
        pl.semaphore_signal(barrier, inc=1, device_id={"tm": tm_to, "space": space_to}, device_id_type=MESH)

    greet(tm, space(0, z, y, 1 - x))

    @pl.loop(1, 16)
    def _(k):
        d = (tm * 4 + z + k) % 16
        greet(d // 4, space(0, d % 4, y, x))

    @pl.loop(0, 12)
    def _(k):
        greet((tm + k // 3) % 4, space(0, z, ring(y, 1 + k % 3), x))

    def remote(src, dst, send_sem, recv_sem, space_to, tm_to=None):
        to = {"space": space_to}
        if tm_to is not None:
            to["tm"] = tm_to
        return pltpu.make_async_remote_copy(
            src_ref=src, dst_ref=dst, send_sem=send_sem, recv_sem=recv_sem, device_id=to, device_id_type=MESH
        )

    def arrived(ref, sem):
        pltpu.make_async_copy(ref, ref, sem).wait()

    tables_in[0].wait()

    def rows_of(j):
        fetch(j).wait()
        block = vbuf[pl.ds(4 * j, 4)].reshape(256, N)
        low, high = block[:, : N // 2], block[:, N // 2 :]
        for half, folded in ((0, low + high), (1, low - high)):
            hi, lo = split(folded)
            out = dot(hi, rows[half, 0]) + dot(lo, rows[half, 0]) + dot(hi, rows[half, 1])
            send1[half, j] = out.reshape(4, 64, 256)

    def send_rows(j):
        for half in range(2):
            a, b = first[half], second[half]
            for d in (1, 3, 2):
                to = ring(a, d)
                remote(
                    send1.at[half, j, to], recv1.at[half, j, a],
                    s1_send.at[half], s1_recv.at[half, j], space(half, to, b, x),
                ).start()
            recv1[half, j, a] = send1[half, j, a]

    rows_of(0)
    pl.semaphore_wait(barrier, 28)
    send_rows(0)

    @pl.loop(1, STEPS)
    def _(j):
        rows_of(j)
        send_rows(j)

    for copy in tables_in[1:]:
        copy.wait()

    @pl.loop(0, STEPS)
    def _(j):
        for half in range(2):
            b = second[half]
            arrived(recv1.at[half, j, pl.ds(0, 3)], s1_recv.at[half, j])
            data = recv1[half, j].reshape(256, 256)
            re, im = turned(cols[half, 0], cols[half, 1], data)
            part[half, j, :, :, :128] = re.reshape(4, 64, 128)
            part[half, j, :, :, 128:] = im.reshape(4, 64, 128)
            far = ring(b, 2)
            for way in range(2):
                to = ring(b, 1 + 2 * way)
                remote(
                    part.at[half, j, far, pl.ds(32 * way, 32)], hrecv.at[half, j, way],
                    h_send.at[half], h_recv.at[half, j], space(half, first[half], to, x),
                ).start()

    @pl.loop(0, STEPS)
    def _(j):
        for half in range(2):
            b = second[half]
            arrived(hrecv.at[half, j], h_recv.at[half, j])
            for way in range(2):
                to = ring(b, 1 + 2 * way)
                at = pl.ds(32 * way, 32)
                part[half, j, to, at] = part[half, j, to, at] + hrecv[half, j, way]
                remote(
                    part.at[half, j, to], qrecv.at[half, j, way],
                    q_send.at[half], q_recv.at[half, j], space(half, first[half], to, x),
                ).start()

    @pl.loop(0, STEPS)
    def _(j):
        for half in range(2):
            b = second[half]
            arrived(qrecv.at[half, j], q_recv.at[half, j])
            for keep, at in ((xsend, pl.ds(32 * (1 - x), 32)), (xkeep, pl.ds(32 * x, 32))):
                keep[half, j] = part[half, j, b, at] + qrecv[half, j, 0, at] + qrecv[half, j, 1, at]
            remote(
                xsend.at[half, j], xrecv.at[half, j],
                x_send.at[half], x_recv.at[half, j], space(half, first[half], b, 1 - x),
            ).start()

    for half in range(2):
        for j in range(STEPS):
            arrived(xrecv.at[half, j], x_recv.at[half, j])
            whole = xkeep[half, j] + xrecv[half, j]
            for d in range(16):
                fsend[half, d, 2 * j : 2 * j + 2] = whole[2 * d : 2 * d + 2]
        a, b = first[half], second[half]
        mine = tm * 4 + a
        frecv[half, mine] = fsend[half, mine]

        @pl.loop(1, 16)
        def _(k):
            d = (mine + k) % 16
            remote(
                fsend.at[half, d], frecv.at[half, mine],
                f_send.at[half], f_recv.at[half], space(half, d % 4, b, x), d // 4,
            ).start()

    power = []
    for half in range(2):
        arrived(frecv.at[half, pl.ds(0, 15)], f_recv.at[half])
        re, im = turned(time[0], time[1], frecv[half].reshape(256, 256))
        power.append(re * re + im * im)
    both = jnp.concatenate(power, axis=1)
    hi, rest = both.astype(BF16), None
    rest = both - hi.astype(F32)
    mid = rest.astype(BF16)
    low = (rest - mid.astype(F32)).astype(BF16)
    o_ref[...] = dot(hi, perm[...]) + dot(mid, perm[...]) + dot(low, perm[...])

    for half in range(2):
        arrived(send1.at[half, :, pl.ds(0, 3)], s1_send.at[half])
        arrived(hrecv.at[half], h_send.at[half])
        arrived(qrecv.at[half], q_send.at[half])
        arrived(xsend.at[half], x_send.at[half])
        arrived(fsend.at[half, pl.ds(0, 15)], f_send.at[half])


def per_device(vorticity):
    any_spec = pl.BlockSpec(memory_space=pl.ANY)
    dma = pltpu.SemaphoreType.DMA
    out = pl.pallas_call(
        kernel,
        out_shape=jax.ShapeDtypeStruct((2 * T_SIZE, K), F32),
        in_specs=[any_spec] * 6,
        out_specs=pl.BlockSpec(memory_space=pltpu.VMEM),
        scratch_shapes=[
            pltpu.VMEM((32, 64, N), F32),
            pltpu.VMEM((2, 2, N // 2, 256), BF16),
            pltpu.VMEM((2, 2, 512, 256), BF16),
            pltpu.VMEM((2, 512, 256), BF16),
            pltpu.VMEM((K, K), BF16),
            pltpu.VMEM((2, STEPS, 4, 64, 256), F32),
            pltpu.VMEM((2, STEPS, 4, 64, 256), F32),
            pltpu.VMEM((2, STEPS, 4, 64, 256), F32),
            pltpu.VMEM((2, STEPS, 2, 32, 256), F32),
            pltpu.VMEM((2, STEPS, 2, 64, 256), F32),
            pltpu.VMEM((2, STEPS, 32, 256), F32),
            pltpu.VMEM((2, STEPS, 32, 256), F32),
            pltpu.VMEM((2, STEPS, 32, 256), F32),
            pltpu.VMEM((2, 16, 16, 256), F32),
            pltpu.VMEM((2, 16, 16, 256), F32),
            dma((STEPS,)),
            dma((5,)),
            dma((2,)), dma((2, STEPS)),
            dma((2,)), dma((2, STEPS)),
            dma((2,)), dma((2, STEPS)),
            dma((2,)), dma((2, STEPS)),
            dma((2,)), dma((2,)),
        ],
        compiler_params=pltpu.CompilerParams(
            collective_id=0, has_side_effects=True, vmem_limit_bytes=60 * 2**20
        ),
        cost_estimate=pl.CostEstimate(flops=12 * 10**9, bytes_accessed=24 * 2**20, transcendentals=0),
    )(vorticity, *(jnp.asarray(t) for t in tables()))
    return out.reshape(T_SIZE, 2, K)


def solution(mesh):
    return jax.shard_map(
        per_device,
        mesh=mesh,
        in_specs=(P("tm", "space", None),),
        out_specs=P(None, ("tm", "space"), None),
        check_vma=False,
    )
```

profile of v0, /device:TPU:1, one launch (start us, length us, event | category | flops | bytes accessed | tf_op | source)
XLA Modules:
  0.0 66.5 jit_solution(4199804201584344040)
XLA Ops:
  0.0 64.7 %shard_map.64 = f32[256,256]{1,0:T(8,128)} custom-call(f32[32,64,2048]{2,1,0:T(8,128)} %v_ref.1, bf16[2,2,1024,256]{3,2,1,0:T(8,128)(2,1)} %constant.10.clone.rows_ref, bf16[8,2,512,256]{3,2,1,0:T(8,128)(2,1)} %constant.11.clone.cola_ref, bf16[8,2,512,256]{3,2,1,0:T(8,128)(2,1)} %constant.12.clone.colb_ref, bf16[2,512,256]{2,1,0:T(8,128)(2,1)} %constant.13.clone.time_ref, ...), custom_call_target="tpu_custom_call" | custom-call | flops 12000000000 | bytes 25165824 | tf_op jit(solution)/shard_map/pallas_call | solution.py:267
  64.7 1.8 %reshape.3 = f32[128,2,256]{2,1,0:T(2,128)} reshape(f32[256,256]{1,0:T(8,128)} %shard_map.64) | data formatting | bytes 524288 | tf_op jit(solution)/shard_map/reshape | solution.py:301
where the time goes:
time: 66.7 us; the launch traced here: 66.5 us
  Pallas kernels  64.7 us (97%)
  local copies, waits for them, and re-layouts  1.8 us (3%)
    pallas_call x1, Pallas kernels, per_device(): pl.pallas_call(kernel, out_shape=jax.ShapeDtypeStruct((2 * T_SIZE, K), F3...  64.7 us
    reshape x1, local copies, waits for them, and re-layouts, per_device(): return out.reshape(T_SIZE, 2, K)  1.8 us

commit v1 on v0

--- a/solution.py
+++ b/solution.py
@@ -15,6 +15,8 @@
 MESH = pl.DeviceIdType.MESH
 F32, BF16 = jnp.float32, jnp.bfloat16
 STEPS = 8
+EARLY, LATE = 4, 4
+LAG, CROSS, GAP = 4, 4, 2
 
 
 def halves(a):
@@ -55,8 +57,8 @@
     t = np.arange(T_SIZE)
     taper = 0.5 - 0.5 * np.cos(2.0 * np.pi * t / T_SIZE)
     scale = taper / N / np.sqrt(np.sum(taper * taper))
-    tm, a, j = np.meshgrid(np.arange(4), np.arange(4), np.arange(8), indexing="ij")
-    when = (32 * tm + 4 * j + a).reshape(-1)
+    group, tm, a, j = np.meshgrid(np.arange(2), np.arange(4), np.arange(4), np.arange(4), indexing="ij")
+    when = (32 * tm + 4 * (4 * group + j) + a).reshape(-1)
     c, s = turn(np.arange(T_SIZE)[:, None] * when[None, :], T_SIZE)
     eye = np.eye(2)
     time = halves(
@@ -87,12 +89,14 @@
 def kernel(
     v_ref, rows_ref, cola_ref, colb_ref, time_ref, perm_ref, o_ref,
     vbuf, rows, cols, time, perm,
-    send1, recv1, part, hrecv, qrecv, xsend, xkeep, xrecv, fsend, frecv,
-    v_sem, c_sem, s1_send, s1_recv, h_send, h_recv, q_send, q_recv, x_send, x_recv, f_send, f_recv,
+    send1, recv1, part, wrecv, erecv, grecv, hrecv, qrecv, xsend, xkeep, xrecv, fsend, frecv,
+    v_sem, c_sem, s1_send, s1_recv, w_send, w_recv, e_send, e_recv, g_send, g_recv,
+    h_send, h_recv, q_send, q_recv, x_send, x_recv, f_send, f_recv, relay,
 ):
     tm = lax.axis_index("tm")
     me = lax.axis_index("space")
     z, y, x = me // 8, (me // 2) % 4, me % 2
+    own, other = pl.ds(32 * x, 32), pl.ds(32 * (1 - x), 32)
     first = (z, y)
     second = (y, z)
 
@@ -114,26 +118,18 @@
         return pltpu.make_async_copy(v_ref.at[pl.ds(4 * j, 4)], vbuf.at[pl.ds(4 * j, 4)], v_sem.at[j])
 
     tables_in[0].start()
-    for j in range(STEPS):
-        fetch(j).start()
-    for copy in tables_in[1:]:
-        copy.start()
+    fetch(0).start()
 
     barrier = pltpu.get_barrier_semaphore()
 
-    def greet(tm_to, space_to):
-        pl.semaphore_signal(barrier, inc=1, device_id={"tm": tm_to, "space": space_to}, device_id_type=MESH)
-
-    greet(tm, space(0, z, y, 1 - x))
-
-    @pl.loop(1, 16)
-    def _(k):
-        d = (tm * 4 + z + k) % 16
-        greet(d // 4, space(0, d % 4, y, x))
-
-    @pl.loop(0, 12)
-    def _(k):
-        greet((tm + k // 3) % 4, space(0, z, ring(y, 1 + k % 3), x))
+    def signal(sem, tm_to, space_to):
+        pl.semaphore_signal(sem, inc=1, device_id={"tm": tm_to, "space": space_to}, device_id_type=MESH)
+
+    for d in (1, 3, 2):
+        signal(barrier, tm, space(0, ring(z, d), y, x))
+        signal(barrier, tm, space(0, z, ring(y, d), x))
+        signal(barrier, ring(tm, d), me)
+    signal(barrier, tm, space(0, z, y, 1 - x))
 
     def remote(src, dst, send_sem, recv_sem, space_to, tm_to=None):
         to = {"space": space_to}
@@ -147,9 +143,13 @@
         pltpu.make_async_copy(ref, ref, sem).wait()
 
     tables_in[0].wait()
+    fetch(0).wait()
+    for j in range(1, STEPS):
+        fetch(j).start()
+    for copy in tables_in[1:]:
+        copy.start()
 
     def rows_of(j):
-        fetch(j).wait()
         block = vbuf[pl.ds(4 * j, 4)].reshape(256, N)
         low, high = block[:, : N // 2], block[:, N // 2 :]
         for half, folded in ((0, low + high), (1, low - high)):
@@ -169,81 +169,156 @@
             recv1[half, j, a] = send1[half, j, a]
 
     rows_of(0)
-    pl.semaphore_wait(barrier, 28)
+    pl.semaphore_wait(barrier, 10)
     send_rows(0)
-
-    @pl.loop(1, STEPS)
-    def _(j):
-        rows_of(j)
-        send_rows(j)
-
-    for copy in tables_in[1:]:
-        copy.wait()
-
-    @pl.loop(0, STEPS)
-    def _(j):
-        for half in range(2):
-            b = second[half]
+    for d in (1, 3, 2):
+        signal(relay, ring(tm, d), me)
+
+    def columns_of(j):
+        for half in range(2):
             arrived(recv1.at[half, j, pl.ds(0, 3)], s1_recv.at[half, j])
             data = recv1[half, j].reshape(256, 256)
             re, im = turned(cols[half, 0], cols[half, 1], data)
             part[half, j, :, :, :128] = re.reshape(4, 64, 128)
             part[half, j, :, :, 128:] = im.reshape(4, 64, 128)
-            far = ring(b, 2)
-            for way in range(2):
-                to = ring(b, 1 + 2 * way)
-                remote(
-                    part.at[half, j, far, pl.ds(32 * way, 32)], hrecv.at[half, j, way],
-                    h_send.at[half], h_recv.at[half, j], space(half, first[half], to, x),
-                ).start()
-
-    @pl.loop(0, STEPS)
-    def _(j):
-        for half in range(2):
-            b = second[half]
+
+    def send_raw(j):
+        for half in range(2):
+            remote(
+                part.at[half, j, :, other], wrecv.at[half, j],
+                w_send.at[half], w_recv.at[half, j], space(half, first[half], second[half], 1 - x),
+            ).start()
+
+    def send_far(half, j, start, rows, dst, send_sem, recv_sem):
+        b = second[half]
+        for way in range(2):
+            remote(
+                part.at[half, j, ring(b, 2), pl.ds(start + rows * way, rows)], dst.at[way],
+                send_sem.at[half], recv_sem, space(half, first[half], ring(b, 1 + 2 * way), x),
+            ).start()
+
+    def send_near(half, j, start, rows, got, dst, send_sem, recv_sem):
+        b = second[half]
+        for way in range(2):
+            to = ring(b, 1 + 2 * way)
+            at = pl.ds(start + rows * way, rows)
+            part[half, j, to, at] = part[half, j, to, at] + got[way]
+            remote(
+                part.at[half, j, to, pl.ds(start, 2 * rows)], dst.at[way],
+                send_sem.at[half], recv_sem, space(half, first[half], to, x),
+            ).start()
+
+    def early_far(j):
+        for half in range(2):
+            arrived(wrecv.at[half, j], w_recv.at[half, j])
+            part[half, j, :, own] = part[half, j, :, own] + wrecv[half, j]
+            send_far(half, j, 32 * x, 16, erecv.at[half, j], e_send, e_recv.at[half, j])
+
+    def early_near(j):
+        for half in range(2):
+            arrived(erecv.at[half, j], e_recv.at[half, j])
+            send_near(half, j, 32 * x, 16, erecv[half, j], grecv.at[half, j], g_send, g_recv.at[half, j])
+
+    def late_near(j):
+        for half in range(2):
             arrived(hrecv.at[half, j], h_recv.at[half, j])
-            for way in range(2):
-                to = ring(b, 1 + 2 * way)
-                at = pl.ds(32 * way, 32)
-                part[half, j, to, at] = part[half, j, to, at] + hrecv[half, j, way]
-                remote(
-                    part.at[half, j, to], qrecv.at[half, j, way],
-                    q_send.at[half], q_recv.at[half, j], space(half, first[half], to, x),
-                ).start()
-
-    @pl.loop(0, STEPS)
-    def _(j):
+            send_near(half, j + EARLY, 0, 32, hrecv[half, j], qrecv.at[half, j], q_send, q_recv.at[half, j])
+
+    def late_sum(j):
         for half in range(2):
             b = second[half]
             arrived(qrecv.at[half, j], q_recv.at[half, j])
-            for keep, at in ((xsend, pl.ds(32 * (1 - x), 32)), (xkeep, pl.ds(32 * x, 32))):
-                keep[half, j] = part[half, j, b, at] + qrecv[half, j, 0, at] + qrecv[half, j, 1, at]
+            for keep, at in ((xsend, other), (xkeep, own)):
+                keep[half, j] = part[half, j + EARLY, b, at] + qrecv[half, j, 0, at] + qrecv[half, j, 1, at]
             remote(
                 xsend.at[half, j], xrecv.at[half, j],
                 x_send.at[half], x_recv.at[half, j], space(half, first[half], b, 1 - x),
             ).start()
 
-    for half in range(2):
-        for j in range(STEPS):
-            arrived(xrecv.at[half, j], x_recv.at[half, j])
-            whole = xkeep[half, j] + xrecv[half, j]
-            for d in range(16):
-                fsend[half, d, 2 * j : 2 * j + 2] = whole[2 * d : 2 * d + 2]
+    def staged(i, part_of, start, count):
+        @pl.when((i >= start) & (i < start + count))
+        def _():
+            part_of(i - start)
+
+    def rows_step(i):
+        fetch(i + 1).wait()
+        rows_of(i + 1)
+        send_rows(i + 1)
+
+    def tables_step(i):
+        for copy in tables_in[1:]:
+            copy.wait()
+
+    def early_columns(j):
+        columns_of(j)
+        send_raw(j)
+
+    def late_columns(j):
+        columns_of(j + EARLY)
+        for half in range(2):
+            send_far(half, j + EARLY, 0, 32, hrecv.at[half, j], h_send, h_recv.at[half, j])
+
+    late = LAG + EARLY
+
+    @pl.loop(1, LAG + STEPS)
+    def _(i):
+        staged(i, rows_step, 1, STEPS - 1)
+        staged(i, tables_step, LAG, 1)
+        staged(i, early_columns, LAG, EARLY)
+        staged(i, late_columns, late, LATE)
+        staged(i, lambda j: early_far(0), LAG + 4, 1)
+        staged(i, lambda j: early_far(1), LAG + 6, 1)
+
+    early_far(2)
+    late_near(0)
+    late_near(1)
+    late_near(2)
+    early_near(0)
+    early_near(1)
+    late_near(3)
+    early_near(2)
+    late_sum(0)
+    late_sum(1)
+    early_far(3)
+    late_sum(2)
+    late_sum(3)
+    early_near(3)
+
+    pl.semaphore_wait(relay, 3)
+
+    def lay_out(half, group, j, whole):
+        for d in range(16):
+            fsend[half, group, d, 2 * j : 2 * j + 2] = whole[2 * d : 2 * d + 2]
+
+    def send_owned(half, group):
         a, b = first[half], second[half]
         mine = tm * 4 + a
-        frecv[half, mine] = fsend[half, mine]
+        frecv[half, group, mine] = fsend[half, group, mine]
 
         @pl.loop(1, 16)
         def _(k):
             d = (mine + k) % 16
             remote(
-                fsend.at[half, d], frecv.at[half, mine],
-                f_send.at[half], f_recv.at[half], space(half, d % 4, b, x), d // 4,
-            ).start()
+                fsend.at[half, group, d], frecv.at[half, group, mine],
+                f_send.at[half], f_recv.at[half, group], space(half, d % 4, b, x), d // 4,
+            ).start()
+
+    for group in (1, 0):
+        for half in range(2):
+            for j in range(4 * group, 4 * group + 4):
+                if j < EARLY:
+                    arrived(grecv.at[half, j], g_recv.at[half, j])
+                    whole = part[half, j, second[half], own] + grecv[half, j, 0] + grecv[half, j, 1]
+                else:
+                    arrived(xrecv.at[half, j - EARLY], x_recv.at[half, j - EARLY])
+                    whole = xkeep[half, j - EARLY] + xrecv[half, j - EARLY]
+                lay_out(half, group, j % 4, whole)
+            send_owned(half, group)
 
     power = []
     for half in range(2):
-        arrived(frecv.at[half, pl.ds(0, 15)], f_recv.at[half])
+        for group in range(2):
+            arrived(frecv.at[half, group, pl.ds(0, 15)], f_recv.at[half, group])
         re, im = turned(time[0], time[1], frecv[half].reshape(256, 256))
         power.append(re * re + im * im)
     both = jnp.concatenate(power, axis=1)
@@ -255,10 +330,13 @@
 
     for half in range(2):
         arrived(send1.at[half, :, pl.ds(0, 3)], s1_send.at[half])
+        arrived(wrecv.at[half], w_send.at[half])
+        arrived(erecv.at[half], e_send.at[half])
+        arrived(grecv.at[half], g_send.at[half])
         arrived(hrecv.at[half], h_send.at[half])
         arrived(qrecv.at[half], q_send.at[half])
         arrived(xsend.at[half], x_send.at[half])
-        arrived(fsend.at[half, pl.ds(0, 15)], f_send.at[half])
+        arrived(fsend.at[half, :, pl.ds(0, 15)], f_send.at[half])
 
 
 def per_device(vorticity):
@@ -278,20 +356,27 @@
             pltpu.VMEM((2, STEPS, 4, 64, 256), F32),
             pltpu.VMEM((2, STEPS, 4, 64, 256), F32),
             pltpu.VMEM((2, STEPS, 4, 64, 256), F32),
-            pltpu.VMEM((2, STEPS, 2, 32, 256), F32),
-            pltpu.VMEM((2, STEPS, 2, 64, 256), F32),
-            pltpu.VMEM((2, STEPS, 32, 256), F32),
-            pltpu.VMEM((2, STEPS, 32, 256), F32),
-            pltpu.VMEM((2, STEPS, 32, 256), F32),
-            pltpu.VMEM((2, 16, 16, 256), F32),
-            pltpu.VMEM((2, 16, 16, 256), F32),
+            pltpu.VMEM((2, EARLY, 4, 32, 256), F32),
+            pltpu.VMEM((2, EARLY, 2, 16, 256), F32),
+            pltpu.VMEM((2, EARLY, 2, 32, 256), F32),
+            pltpu.VMEM((2, LATE, 2, 32, 256), F32),
+            pltpu.VMEM((2, LATE, 2, 64, 256), F32),
+            pltpu.VMEM((2, LATE, 32, 256), F32),
+            pltpu.VMEM((2, LATE, 32, 256), F32),
+            pltpu.VMEM((2, LATE, 32, 256), F32),
+            pltpu.VMEM((2, 2, 16, 8, 256), F32),
+            pltpu.VMEM((2, 2, 16, 8, 256), F32),
             dma((STEPS,)),
             dma((5,)),
             dma((2,)), dma((2, STEPS)),
-            dma((2,)), dma((2, STEPS)),
-            dma((2,)), dma((2, STEPS)),
-            dma((2,)), dma((2, STEPS)),
-            dma((2,)), dma((2,)),
+            dma((2,)), dma((2, EARLY)),
+            dma((2,)), dma((2, EARLY)),
+            dma((2,)), dma((2, EARLY)),
+            dma((2,)), dma((2, LATE)),
+            dma((2,)), dma((2, LATE)),
+            dma((2,)), dma((2, LATE)),
+            dma((2,)), dma((2, 2)),
+            pltpu.SemaphoreType.REGULAR,
         ],
         compiler_params=pltpu.CompilerParams(
             collective_id=0, has_side_effects=True, vmem_limit_bytes=60 * 2**20

time: 66.7 us -> 60.4 us (0.906)
  Pallas kernels: 64.7 us -> 58.4 us
    pallas_call x1, Pallas kernels: 64.7 us -> 58.4 us  [per_device(): pl.pallas_call(kernel, out_shape=jax.ShapeDtypeStruct((2 * T_SIZE, K), F3...]
where the time goes in v1:
time: 60.4 us; the launch traced here: 60.2 us
  Pallas kernels  58.4 us (97%)
  local copies, waits for them, and re-layouts  1.8 us (3%)
    pallas_call x1, Pallas kernels, per_device(): pl.pallas_call(kernel, out_shape=jax.ShapeDtypeStruct((2 * T_SIZE, K), F3...  58.4 us
    reshape x1, local copies, waits for them, and re-layouts, per_device(): return out.reshape(T_SIZE, 2, K)  1.8 us

profile of v1, /device:TPU:1, one launch (start us, length us, event | category | flops | bytes accessed | tf_op | source)
XLA Modules:
  0.0 60.2 jit_solution(411893503332374252)
XLA Ops:
  0.0 58.4 %shard_map.64 = f32[256,256]{1,0:T(8,128)} custom-call(f32[32,64,2048]{2,1,0:T(8,128)} %v_ref.1, bf16[2,2,1024,256]{3,2,1,0:T(8,128)(2,1)} %constant.10.clone.rows_ref, bf16[8,2,512,256]{3,2,1,0:T(8,128)(2,1)} %constant.11.clone.cola_ref, bf16[8,2,512,256]{3,2,1,0:T(8,128)(2,1)} %constant.12.clone.colb_ref, bf16[2,512,256]{2,1,0:T(8,128)(2,1)} %constant.13.clone.time_ref, ...), custom_call_target="tpu_custom_call" | custom-call | flops 12000000000 | bytes 25165824 | tf_op jit(solution)/shard_map/pallas_call | solution.py:345
  58.4 1.8 %reshape.3 = f32[128,2,256]{2,1,0:T(2,128)} reshape(f32[256,256]{1,0:T(8,128)} %shard_map.64) | data formatting | bytes 524288 | tf_op jit(solution)/shard_map/reshape | solution.py:386

commit v2 on v1

--- a/solution.py
+++ b/solution.py
@@ -57,13 +57,15 @@
     t = np.arange(T_SIZE)
     taper = 0.5 - 0.5 * np.cos(2.0 * np.pi * t / T_SIZE)
     scale = taper / N / np.sqrt(np.sum(taper * taper))
-    group, tm, a, j = np.meshgrid(np.arange(2), np.arange(4), np.arange(4), np.arange(4), indexing="ij")
-    when = (32 * tm + 4 * (4 * group + j) + a).reshape(-1)
+    group, tm, a, j = np.meshgrid(
+        np.arange(STEPS // 2), np.arange(4), np.arange(4), np.arange(2), indexing="ij"
+    )
+    when = (32 * tm + 4 * (2 * group + j) + a).reshape(-1)
     c, s = turn(np.arange(T_SIZE)[:, None] * when[None, :], T_SIZE)
+    c, s = ((v * scale[when]).reshape(T_SIZE, -1, 1, 2) for v in (c, s))
+    sides = [np.concatenate(pair, axis=2).reshape(T_SIZE, -1) for pair in ((c, s), (-s, c))]
     eye = np.eye(2)
-    time = halves(
-        np.concatenate([np.kron(c * scale[when], eye), np.kron(s * scale[when], eye)], axis=0)
-    )
+    time = halves(np.concatenate([np.kron(side, eye) for side in sides], axis=0))
     perm = np.zeros((K, K))
     k = np.arange(K)
     perm[(k % 2) * 128 + k // 2, k] = 1.0
@@ -269,6 +271,34 @@
         staged(i, lambda j: early_far(0), LAG + 4, 1)
         staged(i, lambda j: early_far(1), LAG + 6, 1)
 
+    def send_owned(group):
+        for half in range(2):
+            for j in range(2):
+                n = 2 * group + j
+                if n < EARLY:
+                    arrived(grecv.at[half, n], g_recv.at[half, n])
+                    whole = part[half, n, second[half], own] + grecv[half, n, 0] + grecv[half, n, 1]
+                else:
+                    n = n - EARLY
+                    arrived(xrecv.at[half, n], x_recv.at[half, n])
+                    whole = xkeep[half, n] + xrecv[half, n]
+                for d in range(16):
+                    for side in range(2):
+                        fsend[half, group, d, 4 * side + 2 * j : 4 * side + 2 * j + 2] = whole[
+                            2 * d : 2 * d + 2, 128 * side : 128 * side + 128
+                        ]
+            a, b = first[half], second[half]
+            mine = tm * 4 + a
+            frecv[half, group, mine] = fsend[half, group, mine]
+
+            @pl.loop(1, 16)
+            def _(k):
+                d = (mine + k) % 16
+                remote(
+                    fsend.at[half, group, d], frecv.at[half, group, mine],
+                    f_send.at[half], f_recv.at[half, group], space(half, d % 4, b, x), d // 4,
+                ).start()
+
     early_far(2)
     late_near(0)
     late_near(1)
@@ -279,50 +309,22 @@
     early_near(2)
     late_sum(0)
     late_sum(1)
+    pl.semaphore_wait(relay, 3)
     early_far(3)
     late_sum(2)
     late_sum(3)
     early_near(3)
-
-    pl.semaphore_wait(relay, 3)
-
-    def lay_out(half, group, j, whole):
-        for d in range(16):
-            fsend[half, group, d, 2 * j : 2 * j + 2] = whole[2 * d : 2 * d + 2]
-
-    def send_owned(half, group):
-        a, b = first[half], second[half]
-        mine = tm * 4 + a
-        frecv[half, group, mine] = fsend[half, group, mine]
-
-        @pl.loop(1, 16)
-        def _(k):
-            d = (mine + k) % 16
-            remote(
-                fsend.at[half, group, d], frecv.at[half, group, mine],
-                f_send.at[half], f_recv.at[half, group], space(half, d % 4, b, x), d // 4,
-            ).start()
-
-    for group in (1, 0):
-        for half in range(2):
-            for j in range(4 * group, 4 * group + 4):
-                if j < EARLY:
-                    arrived(grecv.at[half, j], g_recv.at[half, j])
-                    whole = part[half, j, second[half], own] + grecv[half, j, 0] + grecv[half, j, 1]
-                else:
-                    arrived(xrecv.at[half, j - EARLY], x_recv.at[half, j - EARLY])
-                    whole = xkeep[half, j - EARLY] + xrecv[half, j - EARLY]
-                lay_out(half, group, j % 4, whole)
-            send_owned(half, group)
-
-    power = []
+    send_owned(0)
+    send_owned(2)
+    send_owned(3)
+    send_owned(1)
     for half in range(2):
-        for group in range(2):
+        for group in range(STEPS // 2):
             arrived(frecv.at[half, group, pl.ds(0, 15)], f_recv.at[half, group])
-        re, im = turned(time[0], time[1], frecv[half].reshape(256, 256))
-        power.append(re * re + im * im)
-    both = jnp.concatenate(power, axis=1)
-    hi, rest = both.astype(BF16), None
+    hi, lo = split(jnp.concatenate([frecv[half].reshape(512, 128) for half in range(2)], axis=1))
+    sums = dot(time[0], hi) + dot(time[0], lo) + dot(time[1], hi)
+    both = sums[:256] * sums[:256] + sums[256:] * sums[256:]
+    hi = both.astype(BF16)
     rest = both - hi.astype(F32)
     mid = rest.astype(BF16)
     low = (rest - mid.astype(F32)).astype(BF16)
@@ -351,7 +353,7 @@
             pltpu.VMEM((32, 64, N), F32),
             pltpu.VMEM((2, 2, N // 2, 256), BF16),
             pltpu.VMEM((2, 2, 512, 256), BF16),
-            pltpu.VMEM((2, 512, 256), BF16),
+            pltpu.VMEM((2, 512, 512), BF16),
             pltpu.VMEM((K, K), BF16),
             pltpu.VMEM((2, STEPS, 4, 64, 256), F32),
             pltpu.VMEM((2, STEPS, 4, 64, 256), F32),
@@ -364,8 +366,8 @@
             pltpu.VMEM((2, LATE, 32, 256), F32),
             pltpu.VMEM((2, LATE, 32, 256), F32),
             pltpu.VMEM((2, LATE, 32, 256), F32),
-            pltpu.VMEM((2, 2, 16, 8, 256), F32),
-            pltpu.VMEM((2, 2, 16, 8, 256), F32),
+            pltpu.VMEM((2, STEPS // 2, 16, 8, 128), F32),
+            pltpu.VMEM((2, STEPS // 2, 16, 8, 128), F32),
             dma((STEPS,)),
             dma((5,)),
             dma((2,)), dma((2, STEPS)),
@@ -375,7 +377,7 @@
             dma((2,)), dma((2, LATE)),
             dma((2,)), dma((2, LATE)),
             dma((2,)), dma((2, LATE)),
-            dma((2,)), dma((2, 2)),
+            dma((2,)), dma((2, STEPS // 2)),
             pltpu.SemaphoreType.REGULAR,
         ],
         compiler_params=pltpu.CompilerParams(

time: 60.4 us -> 59.5 us (0.985)
  Pallas kernels: 58.4 us -> 57.6 us
    pallas_call x1, Pallas kernels: 58.4 us -> 57.6 us  [per_device(): pl.pallas_call(kernel, out_shape=jax.ShapeDtypeStruct((2 * T_SIZE, K), F3...]
where the time goes in v2:
time: 59.5 us; the launch traced here: 59.4 us
  Pallas kernels  57.6 us (97%)
  local copies, waits for them, and re-layouts  1.8 us (3%)
    pallas_call x1, Pallas kernels, per_device(): pl.pallas_call(kernel, out_shape=jax.ShapeDtypeStruct((2 * T_SIZE, K), F3...  57.6 us
    reshape x1, local copies, waits for them, and re-layouts, per_device(): return out.reshape(T_SIZE, 2, K)  1.8 us

profile of v2, /device:TPU:1, one launch (start us, length us, event | category | flops | bytes accessed | tf_op | source)
XLA Modules:
  0.0 59.4 jit_solution(16162317403814323127)
XLA Ops:
  0.0 57.6 %shard_map.64 = f32[256,256]{1,0:T(8,128)} custom-call(f32[32,64,2048]{2,1,0:T(8,128)} %v_ref.1, bf16[2,2,1024,256]{3,2,1,0:T(8,128)(2,1)} %constant.10.clone.rows_ref, bf16[8,2,512,256]{3,2,1,0:T(8,128)(2,1)} %constant.11.clone.cola_ref, bf16[8,2,512,256]{3,2,1,0:T(8,128)(2,1)} %constant.12.clone.colb_ref, bf16[2,512,512]{2,1,0:T(8,128)(2,1)} %constant.13.clone.time_ref, ...), custom_call_target="tpu_custom_call" | custom-call | flops 12000000000 | bytes 25165824 | tf_op jit(solution)/shard_map/pallas_call | solution.py:347
  57.6 1.8 %reshape.3 = f32[128,2,256]{2,1,0:T(2,128)} reshape(f32[256,256]{1,0:T(8,128)} %shard_map.64) | data formatting | bytes 524288 | tf_op jit(solution)/shard_map/reshape | solution.py:388

commit v3 on v2

--- a/solution.py
+++ b/solution.py
@@ -15,6 +15,7 @@
 MESH = pl.DeviceIdType.MESH
 F32, BF16 = jnp.float32, jnp.bfloat16
 STEPS = 8
+ORDER = (0, 2, 3, 1)
 EARLY, LATE = 4, 4
 LAG, CROSS, GAP = 4, 4, 2
 
@@ -58,7 +59,7 @@
     taper = 0.5 - 0.5 * np.cos(2.0 * np.pi * t / T_SIZE)
     scale = taper / N / np.sqrt(np.sum(taper * taper))
     group, tm, a, j = np.meshgrid(
-        np.arange(STEPS // 2), np.arange(4), np.arange(4), np.arange(2), indexing="ij"
+        np.array(ORDER), np.arange(4), np.arange(4), np.arange(2), indexing="ij"
     )
     when = (32 * tm + 4 * (2 * group + j) + a).reshape(-1)
     c, s = turn(np.arange(T_SIZE)[:, None] * when[None, :], T_SIZE)
@@ -119,9 +120,6 @@
     def fetch(j):
         return pltpu.make_async_copy(v_ref.at[pl.ds(4 * j, 4)], vbuf.at[pl.ds(4 * j, 4)], v_sem.at[j])
 
-    tables_in[0].start()
-    fetch(0).start()
-
     barrier = pltpu.get_barrier_semaphore()
 
     def signal(sem, tm_to, space_to):
@@ -132,6 +130,9 @@
         signal(barrier, tm, space(0, z, ring(y, d), x))
         signal(barrier, ring(tm, d), me)
     signal(barrier, tm, space(0, z, y, 1 - x))
+
+    tables_in[0].start()
+    fetch(0).start()
 
     def remote(src, dst, send_sem, recv_sem, space_to, tm_to=None):
         to = {"space": space_to}
@@ -176,20 +177,20 @@
     for d in (1, 3, 2):
         signal(relay, ring(tm, d), me)
 
-    def columns_of(j):
+    def columns_of(j, then):
         for half in range(2):
             arrived(recv1.at[half, j, pl.ds(0, 3)], s1_recv.at[half, j])
             data = recv1[half, j].reshape(256, 256)
             re, im = turned(cols[half, 0], cols[half, 1], data)
             part[half, j, :, :, :128] = re.reshape(4, 64, 128)
             part[half, j, :, :, 128:] = im.reshape(4, 64, 128)
-
-    def send_raw(j):
-        for half in range(2):
-            remote(
-                part.at[half, j, :, other], wrecv.at[half, j],
-                w_send.at[half], w_recv.at[half, j], space(half, first[half], second[half], 1 - x),
-            ).start()
+            then(half, j)
+
+    def send_raw(half, j):
+        remote(
+            part.at[half, j, :, other], wrecv.at[half, j],
+            w_send.at[half], w_recv.at[half, j], space(half, first[half], second[half], 1 - x),
+        ).start()
 
     def send_far(half, j, start, rows, dst, send_sem, recv_sem):
         b = second[half]
@@ -252,13 +253,13 @@
             copy.wait()
 
     def early_columns(j):
-        columns_of(j)
-        send_raw(j)
+        columns_of(j, send_raw)
 
     def late_columns(j):
-        columns_of(j + EARLY)
-        for half in range(2):
-            send_far(half, j + EARLY, 0, 32, hrecv.at[half, j], h_send, h_recv.at[half, j])
+        columns_of(
+            j + EARLY,
+            lambda half, n: send_far(half, n, 0, 32, hrecv.at[half, j], h_send, h_recv.at[half, j]),
+        )
 
     late = LAG + EARLY
 
@@ -271,7 +272,8 @@
         staged(i, lambda j: early_far(0), LAG + 4, 1)
         staged(i, lambda j: early_far(1), LAG + 6, 1)
 
-    def send_owned(group):
+    def send_owned(slot):
+        group = ORDER[slot]
         for half in range(2):
             for j in range(2):
                 n = 2 * group + j
@@ -284,19 +286,19 @@
                     whole = xkeep[half, n] + xrecv[half, n]
                 for d in range(16):
                     for side in range(2):
-                        fsend[half, group, d, 4 * side + 2 * j : 4 * side + 2 * j + 2] = whole[
+                        fsend[half, slot, d, 4 * side + 2 * j : 4 * side + 2 * j + 2] = whole[
                             2 * d : 2 * d + 2, 128 * side : 128 * side + 128
                         ]
             a, b = first[half], second[half]
             mine = tm * 4 + a
-            frecv[half, group, mine] = fsend[half, group, mine]
+            frecv[half, slot, mine] = fsend[half, slot, mine]
 
             @pl.loop(1, 16)
             def _(k):
                 d = (mine + k) % 16
                 remote(
-                    fsend.at[half, group, d], frecv.at[half, group, mine],
-                    f_send.at[half], f_recv.at[half, group], space(half, d % 4, b, x), d // 4,
+                    fsend.at[half, slot, d], frecv.at[half, slot, mine],
+                    f_send.at[half], f_recv.at[half, slot], space(half, d % 4, b, x), d // 4,
                 ).start()
 
     early_far(2)
@@ -315,14 +317,19 @@
     late_sum(3)
     early_near(3)
     send_owned(0)
+    send_owned(1)
     send_owned(2)
     send_owned(3)
-    send_owned(1)
-    for half in range(2):
-        for group in range(STEPS // 2):
-            arrived(frecv.at[half, group, pl.ds(0, 15)], f_recv.at[half, group])
-    hi, lo = split(jnp.concatenate([frecv[half].reshape(512, 128) for half in range(2)], axis=1))
-    sums = dot(time[0], hi) + dot(time[0], lo) + dot(time[1], hi)
+    sums = None
+    for pair in range(2):
+        for half in range(2):
+            for slot in (2 * pair, 2 * pair + 1):
+                arrived(frecv.at[half, slot, pl.ds(0, 15)], f_recv.at[half, slot])
+        data = [frecv[half, 2 * pair : 2 * pair + 2].reshape(256, 128) for half in range(2)]
+        hi, lo = split(jnp.concatenate(data, axis=1))
+        at = slice(256 * pair, 256 * pair + 256)
+        term = dot(time[0, :, at], hi) + dot(time[0, :, at], lo) + dot(time[1, :, at], hi)
+        sums = term if sums is None else sums + term
     both = sums[:256] * sums[:256] + sums[256:] * sums[256:]
     hi = both.astype(BF16)
     rest = both - hi.astype(F32)

time: 59.5 us -> 59.7 us (level)
  no operation moved by 1% of the time
where the time goes in v3:
time: 59.7 us; the launch traced here: 59.5 us
  Pallas kernels  57.7 us (97%)
  local copies, waits for them, and re-layouts  1.8 us (3%)
    pallas_call x1, Pallas kernels, per_device(): pl.pallas_call(kernel, out_shape=jax.ShapeDtypeStruct((2 * T_SIZE, K), F3...  57.7 us
    reshape x1, local copies, waits for them, and re-layouts, per_device(): return out.reshape(T_SIZE, 2, K)  1.8 us

profile of v3, /device:TPU:1, one launch (start us, length us, event | category | flops | bytes accessed | tf_op | source)
XLA Modules:
  0.0 59.5 jit_solution(16458833348460645582)
XLA Ops:
  0.0 57.7 %shard_map.64 = f32[256,256]{1,0:T(8,128)} custom-call(f32[32,64,2048]{2,1,0:T(8,128)} %v_ref.1, bf16[2,2,1024,256]{3,2,1,0:T(8,128)(2,1)} %constant.10.clone.rows_ref, bf16[8,2,512,256]{3,2,1,0:T(8,128)(2,1)} %constant.11.clone.cola_ref, bf16[8,2,512,256]{3,2,1,0:T(8,128)(2,1)} %constant.12.clone.colb_ref, bf16[2,512,512]{2,1,0:T(8,128)(2,1)} %constant.13.clone.time_ref, ...), custom_call_target="tpu_custom_call" | custom-call | flops 12000000000 | bytes 25165824 | tf_op jit(solution)/shard_map/pallas_call | solution.py:354
  57.7 1.8 %reshape.3 = f32[128,2,256]{2,1,0:T(2,128)} reshape(f32[256,256]{1,0:T(8,128)} %shard_map.64) | data formatting | bytes 524288 | tf_op jit(solution)/shard_map/reshape | solution.py:395
